TPU v7x, 32 devices: a whole 2x2x4 slice. The times are simulated.
32 devices in a mesh: row: 8 (over z, y), col: 4 (over x, core).
Axes of the slice: x: 2, y: 2, z: 4, core: 2. Of those that a mesh axis runs over, the one named last changes fastest.
Arguments:
- rhs: float32 [32, 65536], P(None, ('row', 'col')), may hold values from -5 to 7
- coords: float32 [3, 65536], P(None, ('row', 'col')), may hold values from 0 to 8, as said below
- nugget: float32 [65536], P(('row', 'col')), may hold values from 1.5 to 3
- near_ids: int32 [128, 3], P(('row', 'col')), may hold values from -1 to 127, as said below
- basis: float32 [7, 128, 65536], P(None, None, ('row', 'col')), may hold values from -6 to 6
Outputs:
- solution: float32 [32, 65536], P(None, ('row', 'col'))
- residual: float32 [32, 65536], P(None, ('row', 'col'))
Inputs may be any that keep to these rules, and one draw needn't show every extreme that they name: `near_ids`: row i lists leaf i and some of the leaves i - 1 to i + 1 inside the range, each at most once, in any order; the other slots hold -1; the first and last leaf of each device's block of 4 list all such leaves inside the range. `coords`: each leaf's points lie in a unit box with an integer corner; consecutive leaves lie in boxes that share a face.
All inputs are finite; a program needn't handle non-finite values.
Results may differ from a plain program's by a relative error of at most 0.0003.
Values sent between devices are 32-bit elements; how exact they have to be, the bound alone decides.
No kernel may reach another device: no remote copies, remote signals or barrier semaphores. Data moves between devices by JAX's collectives and lax.ppermute only.
A program may use at most 128 MiB of HBM per device.

v0:
```python
import functools

import jax
import jax.numpy as jnp
from jax import lax
from jax.experimental import pallas as pl
from jax.experimental.pallas import tpu as pltpu
from jax.sharding import PartitionSpec as P

LEAF = 512
ITERS = 4
WIN = 3
LANES = 128
TILE = 8
LOCAL = 3
CHUNK = 16
FLOPS = 3 * 10**9

root_three = 1.7320508075688772
spacing_factor = 1.6
matern_scale = root_three / (spacing_factor * LEAF ** (-1.0 / 3.0))

BOTH = ("row", "col")
ROWS_COLS = (((1,), (0,)), ((), ()))
ROWS_ROWS = (((1,), (1,)), ((), ()))


def halves(values):
    high = values.astype(jnp.bfloat16)
    low = (values - high.astype(jnp.float32)).astype(jnp.bfloat16)
    return high, low


def stacked(values):
    return jnp.concatenate(halves(values), axis=0)


def product(stack, high, low, dims):
    rows = stack.shape[0] // 2
    main = lax.dot_general(stack, high, dims, preferred_element_type=jnp.float32)
    rest = lax.dot_general(stack[:rows], low, dims, preferred_element_type=jnp.float32)
    return main[:rows] + (main[rows:] + rest)


def row_sum(values):
    return jnp.sum(values, axis=1, keepdims=True)


def in_lanes(columns, shape):
    lane = lax.broadcasted_iota(jnp.int32, shape, 1)
    block = jnp.zeros(shape, jnp.float32)
    for index, column in enumerate(columns):
        block = jnp.where(lane == index, column, block)
    return block


def sums_tile(columns, rows):
    turned = in_lanes(columns, (rows, LANES)).T[:TILE]
    return jnp.concatenate([turned, jnp.zeros((TILE, LANES - rows), jnp.float32)], axis=1)


def level_terms(level, old, cluster):
    columns = [jnp.zeros((level.shape[0], 1), jnp.float32), row_sum(level * level) * (1.0 / cluster)]
    if old is not None:
        columns.append(row_sum(level * old) * (1.0 / cluster))
    return sums_tile(columns, level.shape[0])


def chosen(core, odd, even):
    return jnp.where(core == 1, odd, even)


def whole(memory=pltpu.VMEM):
    return pl.BlockSpec(memory_space=memory)


def call(body, outs, *args, scalars=0, flops=0, limit=32):
    return pl.pallas_call(
        body,
        out_shape=outs,
        in_specs=[whole(pltpu.SMEM)] * scalars + [whole()] * (len(args) - scalars),
        out_specs=[whole()] * len(outs),
        compiler_params=pltpu.CompilerParams(vmem_limit_bytes=limit * 2**20),
        cost_estimate=pl.CostEstimate(flops=flops, bytes_accessed=2**20, transcendentals=0),
    )(*args)


def f32(*shape):
    return jax.ShapeDtypeStruct(shape, jnp.float32)


def bf16(*shape):
    return jax.ShapeDtypeStruct(shape, jnp.bfloat16)


def matrix_rows(rows, lanes):
    square = None
    for axis in range(3):
        spread = rows[:, axis : axis + 1] - lanes[axis : axis + 1]
        square = spread * spread if square is None else square + spread * spread
    square = square * (matern_scale * matern_scale)
    scaled = square * lax.rsqrt(jnp.maximum(square, 1e-30))
    return halves((1.0 + scaled) * jnp.exp(-scaled))


def setup_kernel(lane_ref, sub_ref, basis_ref, high_ref, low_ref, basis_high_ref, basis_low_ref, raw_ref, sem_ref):
    levels, rank, _ = basis_ref.shape
    copies = [pltpu.make_async_copy(basis_ref.at[at], raw_ref.at[at], sem_ref.at[at]) for at in range(levels)]
    for copy in copies:
        copy.start()
    leaves = lane_ref.shape[1] // LEAF
    parts = LEAF // CHUNK

    def one(step, carry):
        matrix = step // parts
        part = step % parts
        pair = matrix >= leaves
        row_leaf = jnp.where(pair, matrix - leaves, matrix)
        col_leaf = jnp.where(pair, matrix - leaves + 1, matrix)
        row_at = pl.multiple_of(row_leaf * LEAF + part * CHUNK, CHUNK)
        col_at = pl.multiple_of(col_leaf * LEAF, LEAF)
        out_at = pl.ds(pl.multiple_of(part * CHUNK, CHUNK), CHUNK)
        values = matrix_rows(sub_ref[pl.ds(row_at, CHUNK)], lane_ref[:, pl.ds(col_at, LEAF)])
        high_ref[matrix, out_at], low_ref[matrix, out_at] = values
        return carry

    lax.fori_loop(0, (2 * leaves - 1) * parts, one, 0, unroll=4)
    for at, copy in enumerate(copies):
        copy.wait()
        here = slice(at * rank, (at + 1) * rank)
        basis_high_ref[here], basis_low_ref[here] = halves(raw_ref[at])


def edge_matrices(core_ref, rows, sub_ref, paired_ref, other_ref, high_ref, low_ref):
    core = core_ref[0]
    leaves = sub_ref.shape[0] // LEAF
    here = slice(rows, rows + 3)
    lanes = [
        chosen(core, paired_ref[here], other_ref[here]),
        chosen(core, other_ref[here], paired_ref[here]),
    ]

    for side in range(2):
        first_row = side * (leaves - 1) * LEAF

        def one(part, carry):
            row_at = pl.multiple_of(first_row + part * CHUNK, CHUNK)
            out_at = pl.ds(pl.multiple_of(part * CHUNK, CHUNK), CHUNK)
            values = matrix_rows(sub_ref[pl.ds(row_at, CHUNK)], lanes[side])
            high_ref[side, out_at], low_ref[side, out_at] = values
            return carry

        lax.fori_loop(0, LEAF // CHUNK, one, 0, unroll=4)


def edges_kernel(core_ref, field_ref, coords_ref, paired_ref, other_ref):
    core = core_ref[0]
    rows, width = field_ref.shape
    pad = jnp.zeros((TILE - 3, LEAF), jnp.float32)
    head = jnp.concatenate([field_ref[:, :LEAF], coords_ref[:, :LEAF], pad], axis=0)
    tail = jnp.concatenate([field_ref[:, width - LEAF :], coords_ref[:, width - LEAF :], pad], axis=0)
    paired_ref[...] = chosen(core, head, tail)
    other_ref[...] = chosen(core, tail, head)


def down_kernel(field_ref, high_ref, low_ref, local_ref, part_ref):
    rank = LANES
    rows, width = field_ref.shape
    half = width // 2
    stack = stacked(field_ref[...])
    for part in range(2):
        points = slice(part * half, (part + 1) * half)
        local_ref[:, part * rank : (part + 1) * rank] = product(
            stack[:, points], high_ref[:rank, points], low_ref[:rank, points], ROWS_ROWS
        )
    all_points = product(stack, high_ref[rank:], low_ref[rank:], ROWS_ROWS)
    local_ref[:, 2 * rank :] = all_points[:, :rank]
    for bit in range(all_points.shape[1] // rank - 1):
        part_ref[bit * rows : (bit + 1) * rows] = all_points[:, (bit + 1) * rank : (bit + 2) * rank]


def leaf_of(ref, leaf):
    return ref[:, leaf * LEAF : (leaf + 1) * LEAF]


def weight_of(place_ref, ids_ref, leaf, offset):
    target = place_ref[0] * ids_ref.shape[0] + leaf + offset
    found = ids_ref[leaf, 0] == target
    for slot in range(1, WIN):
        found = jnp.logical_or(found, ids_ref[leaf, slot] == target)
    return jnp.where(found, 1.0 / (16 * WIN), 0.0)


def inner_kernel(place_ref, ids_ref, field_ref, nugget_ref, high_ref, low_ref, out_ref):
    leaves = ids_ref.shape[0]
    pieces = [stacked(leaf_of(field_ref, leaf)) for leaf in range(leaves)]
    for leaf in range(leaves):
        inside = product(pieces[leaf], high_ref[leaf], low_ref[leaf], ROWS_COLS)
        total = leaf_of(nugget_ref, leaf) * leaf_of(field_ref, leaf) + weight_of(place_ref, ids_ref, leaf, 0) * inside
        if leaf > 0:
            at = leaves + leaf - 1
            before = product(pieces[leaf - 1], high_ref[at], low_ref[at], ROWS_COLS)
            total = total + weight_of(place_ref, ids_ref, leaf, -1) * before
        if leaf < leaves - 1:
            at = leaves + leaf
            after = product(pieces[leaf + 1], high_ref[at], low_ref[at], ROWS_ROWS)
            total = total + weight_of(place_ref, ids_ref, leaf, 1) * after
        out_ref[:, leaf * LEAF : (leaf + 1) * LEAF] = total


def edge_kernel(first, *refs):
    place_ref, core_ref, ids_ref, field_ref, paired_ref, other_ref, high_ref, low_ref, inner_ref = refs[:9]
    local_ref, part_ref = refs[9:11]
    refs = refs[11:]
    if not first:
        direction_ref, image_ref, old_local_ref = refs[:3]
        refs = refs[3:]
    out_ref, message_ref = refs
    core = core_ref[0]
    leaves = ids_ref.shape[0]
    rows, width = field_ref.shape
    before = chosen(core, paired_ref[:rows], other_ref[:rows])
    after = chosen(core, other_ref[:rows], paired_ref[:rows])
    square = with_image = cross = jnp.zeros((rows, 1), jnp.float32)
    for leaf in range(leaves):
        field = leaf_of(field_ref, leaf)
        total = leaf_of(inner_ref, leaf)
        if leaf == 0:
            part = product(stacked(before), high_ref[0], low_ref[0], ROWS_ROWS)
            total = total + weight_of(place_ref, ids_ref, leaf, -1) * part
        if leaf == leaves - 1:
            part = product(stacked(after), high_ref[1], low_ref[1], ROWS_ROWS)
            total = total + weight_of(place_ref, ids_ref, leaf, 1) * part
        out_ref[:, leaf * LEAF : (leaf + 1) * LEAF] = total
        square = square + row_sum(field * field)
        with_image = with_image + row_sum(field * total)
        if not first:
            cross = cross + row_sum(field * leaf_of(image_ref, leaf) + leaf_of(direction_ref, leaf) * total)
    for block in range(LOCAL):
        scale = 1.0 / (LEAF * (2 if block < 2 else 4))
        here = slice(block * LANES, (block + 1) * LANES)
        with_image = with_image + scale * row_sum(local_ref[:, here] * local_ref[:, here])
        if not first:
            cross = cross + scale * row_sum(local_ref[:, here] * old_local_ref[:, here])
    left = part_ref.shape[0]
    message_ref[:left] = part_ref[...]
    message_ref[left:] = sums_tile([square, with_image, cross], rows)


def combine_kernel(first, bit, cluster, *refs):
    refs = list(refs)
    mine_ref, other_ref = refs[:2]
    refs = refs[2:]
    old_ref = None if first else refs.pop(0)
    *level_refs, next_ref, level_ref = refs
    rows = level_ref.shape[0]
    total = mine_ref[...] + other_ref[...]
    level = total[:rows]
    level_ref[...] = level
    old = None if first else old_ref[bit * rows : (bit + 1) * rows]
    tile = total[total.shape[0] - TILE :] + level_terms(level, old, cluster)
    left = total.shape[0] - TILE - rows
    if left:
        next_ref[:left] = total[rows : rows + left]
        next_ref[left:] = tile
    else:
        for index, ref in enumerate(level_refs):
            next_ref[index * rows : (index + 1) * rows] = ref[...]
        next_ref[bit * rows : (bit + 1) * rows] = level
        next_ref[(bit + 1) * rows :] = tile


def up_kernel(first, last, *refs):
    core_ref, high_ref, low_ref, near_ref, field_ref, mine_ref, other_ref, local_ref = refs[:8]
    refs = refs[8:]
    if not first:
        solution_ref, direction_ref, image_ref, old_local_ref, old_ref, state_ref = refs[:6]
        refs = refs[6:]
    new_solution_ref, new_field_ref = refs[:2]
    if not last:
        new_direction_ref, new_image_ref, new_local_ref, new_old_ref, new_state_ref, paired_ref, send_ref = refs[2:]
    core = core_ref[0]
    rows, width = field_ref.shape
    half = width // 2
    crossing = (mine_ref.shape[0] - TILE) // rows
    whole_sums = chosen(core, mine_ref[...], other_ref[...])
    sums = whole_sums[crossing * rows :].T[:rows]
    norm = sums[:, 0:1]
    curve = sums[:, 1:2]
    ratio = jnp.zeros_like(norm)
    if not first:
        ratio = norm / state_ref[:, 0:1]
        curve = curve + ratio * (sums[:, 2:3] + ratio * state_ref[:, 1:2])
    step = norm / curve
    scaled = []
    for bit in range(crossing):
        scaled.append(whole_sums[bit * rows : (bit + 1) * rows] * (1.0 / (width * (2 << bit))))
    one = [local_ref[:, part * LANES : (part + 1) * LANES] * (1.0 / (2 * LEAF)) for part in range(2)]
    two = local_ref[:, 2 * LANES :] * (1.0 / (4 * LEAF))
    for part in range(2):
        points = slice(part * half, (part + 1) * half)
        stack = stacked(jnp.concatenate([one[part], two] + scaled, axis=1))
        image = near_ref[:, points] + product(stack, high_ref[:, points], low_ref[:, points], ROWS_COLS)
        direction = field_ref[:, points]
        if not first:
            image = image + ratio * image_ref[:, points]
            direction = direction + ratio * direction_ref[:, points]
        moved = step * direction
        new_solution_ref[:, points] = moved if first else solution_ref[:, points] + moved
        new_field_ref[:, points] = field_ref[:, points] - step * image
        if not last:
            new_direction_ref[:, points] = direction
            new_image_ref[:, points] = image
    if not last:
        head = new_field_ref[:, :LEAF]
        tail = new_field_ref[:, width - LEAF :]
        paired_ref[...] = chosen(core, head, tail)
        send_ref[...] = chosen(core, tail, head)
        skeletons = whole_sums[: crossing * rows]
        if first:
            new_local_ref[...] = local_ref[...]
            new_old_ref[...] = skeletons
        else:
            new_local_ref[...] = local_ref[...] + ratio * old_local_ref[...]
            new_old_ref[...] = skeletons + jnp.concatenate([ratio] * crossing, axis=0) * old_ref[...]
        new_state_ref[...] = in_lanes([norm, curve], (rows, LANES))


def per_device(rhs, coords, nugget, near_ids, basis):
    rows, width = rhs.shape
    levels = basis.shape[0]
    leaves = width // LEAF
    crossing = levels - (leaves.bit_length() - 1)
    devices = lax.axis_size("row") * lax.axis_size("col")
    place = jnp.reshape(lax.axis_index(BOTH), (1,))
    core = place % 2

    even = range(0, devices, 2)

    def send(value, pairs):
        return lax.ppermute(value, BOTH, pairs)

    def halo(paired, other):
        outward = [(index, index + 1) for index in range(1, devices - 1, 2)]
        inside = [(index, index ^ 1) for index in range(devices)]
        return send(paired, inside), send(other, outward + [(target, source) for source, target in outward])

    edges = call(edges_kernel, [f32(rows + TILE, LEAF)] * 2, core, rhs, coords, scalars=1)
    edges = halo(*edges)
    turned = coords.T
    *inner_pair, high, low = pl.pallas_call(
        setup_kernel,
        out_shape=[bf16(2 * leaves - 1, LEAF, LEAF)] * 2 + [bf16(levels * LANES, width)] * 2,
        in_specs=[whole(), whole(), whole(pltpu.HBM)],
        out_specs=[whole()] * 4,
        scratch_shapes=[pltpu.VMEM(basis.shape, jnp.float32), pltpu.SemaphoreType.DMA((levels,))],
        compiler_params=pltpu.CompilerParams(vmem_limit_bytes=40 * 2**20),
        cost_estimate=pl.CostEstimate(flops=4 * FLOPS, bytes_accessed=2**20, transcendentals=0),
    )(coords, turned, basis)
    edge_pair = call(
        lambda core_ref, *refs: edge_matrices(core_ref, rows, *refs),
        [bf16(2, LEAF, LEAF)] * 2,
        core,
        turned,
        *edges,
        scalars=1,
        flops=FLOPS,
    )
    nugget = nugget[None, :]

    solution, field, carried = None, rhs, None
    for step in range(ITERS):
        first, last = step == 0, step == ITERS - 1
        local, part = call(
            down_kernel,
            [f32(rows, LOCAL * LANES), f32(crossing * rows, LANES)],
            field,
            high,
            low,
            flops=FLOPS,
        )
        (inner,) = call(
            inner_kernel, [f32(rows, width)], place, near_ids, field, nugget, *inner_pair, scalars=2, flops=FLOPS
        )
        args = [place, core, near_ids, field, *edges, *edge_pair, inner, local, part]
        near, message = call(
            functools.partial(edge_kernel, first),
            [f32(rows, width), f32(crossing * rows + TILE, LANES)],
            *args,
            *([] if first else carried[:3]),
            scalars=3,
            flops=FLOPS // 4,
        )
        done = []
        for bit in range(crossing):
            left = crossing - bit - 1
            if bit == 0:
                got = send(message, [(index, index + 1) for index in even])
            else:
                got = send(message, [(index + 1, (index + 1) ^ (1 << bit)) for index in even])
            args = [message, got] + ([] if first else [carried[3]]) + (done if left == 0 else [])
            message, level = call(
                functools.partial(combine_kernel, first, bit, width * (2 << bit)),
                [f32((left or crossing) * rows + TILE, LANES), f32(rows, LANES)],
                *args,
            )
            done.append(level)
        got = send(message, [(index + 1, index) for index in even])
        args = [core, high, low, near, field, message, got, local]
        if not first:
            args = args + [solution, *carried]
        outs = [f32(rows, width)] * 2
        if not last:
            outs = outs + [f32(rows, width)] * 2 + [f32(rows, LOCAL * LANES), f32(crossing * rows, LANES)]
            outs = outs + [f32(rows, LANES)] + [f32(rows, LEAF)] * 2
        out = call(functools.partial(up_kernel, first, last), outs, *args, scalars=1, flops=FLOPS // 2)
        solution, field = out[:2]
        if not last:
            carried = out[2:7]
            edges = halo(*out[7:9])
    return (solution, field)


def solution(mesh):
    placed = (
        P(None, BOTH),
        P(None, BOTH),
        P(BOTH),
        P(BOTH, None),
        P(None, None, BOTH),
    )
    return jax.shard_map(
        per_device,
        mesh=mesh,
        in_specs=placed,
        out_specs=(P(None, BOTH), P(None, BOTH)),
        check_vma=False,
    )
```

profile of v0, /device:TPU:0, one launch (start us, length us, event | category | flops | bytes accessed | tf_op | source)
XLA Modules:
  0.0 178.9 jit_solution(10231997865525195205)
XLA Ops:
  5.4 12.8 %shard_map.68 = (bf16[7,512,512]{2,1,0:T(8,128)(2,1)S(1)}, bf16[7,512,512]{2,1,0:T(8,128)(2,1)S(1)}, bf16[896,2048]{1,0:T(8,128)(2,1)S(1)}, bf16[896,2048]{1,0:T(8,128)(2,1)}) custom-call(f32[3,2048]{1,0:T(4,128)S(1)} %copy-done.5, f32[2048,3]{1,0:T(8,128)S(1)} %bitcast.3, f32[7,128,2048]{2,1,0:T(8,128)} %basis_ref.1), custom_call_target="tpu_custom_call" | custom-call | flops 12000000000 | bytes 1048576 | tf_op jit(solution)/shard_map/pallas_call | solution.py:351
  18.3 2.0 %copy-done = bf16[896,2048]{1,0:T(8,128)(2,1)S(1)} copy-done((bf16[896,2048]{1,0:T(8,128)(2,1)S(1)}, bf16[896,2048]{1,0:T(8,128)(2,1)}, u32[]{:S(2)}) %copy-start) | copy-done | bytes 3670040
  20.3 2.3 %shard_map.72 = (f32[32,384]{1,0:T(8,128)S(1)}, f32[160,128]{1,0:T(8,128)S(1)}) custom-call(f32[32,2048]{1,0:T(8,128)S(1)} %copy-done.3, bf16[896,2048]{1,0:T(8,128)(2,1)S(1)} %get-tuple-element.89.high_ref.refs_1_, bf16[896,2048]{1,0:T(8,128)(2,1)S(1)} %copy-done), custom_call_target="tpu_custom_call" | custom-call | flops 3000000000 | bytes 1048576 | tf_op jit(solution)/shard_map/pallas_call | solution.py:78
  22.7 2.9 %shard_map.71.refs_8_ = f32[32,2048]{1,0:T(8,128)S(1)} custom-call(s32[1]{0:T(128)} %bitcast.place_ref.refs_0_, s32[4,3]{1,0:T(4,128)S(1)} %copy-done.6, f32[32,2048]{1,0:T(8,128)S(1)} %copy-done.3, f32[1,2048]{1,0:T(1,128)S(1)} %bitcast.5, bf16[7,512,512]{2,1,0:T(8,128)(2,1)S(1)} %get-tuple-element.95.high_ref, ...), custom_call_target="tpu_custom_call" | custom-call | flops 3000000000 | bytes 1048576 | tf_op jit(solution)/shard_map/pallas_call | solution.py:78
  25.6 2.7 %shard_map.70 = (bf16[2,512,512]{2,1,0:T(8,128)(2,1)S(1)}, bf16[2,512,512]{2,1,0:T(8,128)(2,1)S(1)}) custom-call(s32[1]{0:T(128)S(6)} %select_n.7.core_ref.refs_1_.refs_0_, f32[2048,3]{1,0:T(8,128)S(1)} %bitcast.4, f32[40,512]{1,0:T(8,128)S(1)} %collective-permute-done.refs_1_.refs_4_, f32[40,512]{1,0:T(8,128)S(1)} %collective-permute-done.1.refs_2_.refs_5_), custom_call_target="tpu_custom_call" | custom-call | flops 3000000000 | bytes 1048576 | tf_op jit(solution)/shard_map/pallas_call | solution.py:78
  28.3 1.5 shard_map.73
  29.7 5.8 %collective-permute-start.2 = (f32[168,128]{1,0:T(8,128)S(1)}, f32[168,128]{1,0:T(8,128)S(1)}, u32[]{:S(2)}, u32[]{:S(2)}) collective-permute-start(f32[168,128]{1,0:T(8,128)S(1)} %get-tuple-element.100.refs_0_), channel_id=1, source_target_pairs={{0,1},{2,3},{4,5},{6,7},{8,9},{10,11},{12,13},{14,15},{16,17},{18,... | collective-permute-start | bytes 258056 | tf_op jit(solution)/shard_map/ppermute | solution.py:341
  41.6 18.6 %collective-permute-done.7.refs_6_ = f32[168,128]{1,0:T(8,128)S(1)} collective-permute-done((f32[168,128]{1,0:T(8,128)S(1)}, f32[168,128]{1,0:T(8,128)S(1)}, u32[]{:S(2)}, u32[]{:S(2)}) %collective-permute-start.7) | collective-permute-done | bytes 86048 | tf_op jit(solution)/shard_map/ppermute | solution.py:341
  62.5 2.3 %shard_map.81 = (f32[32,384]{1,0:T(8,128)S(1)}, f32[160,128]{1,0:T(8,128)S(1)}) custom-call(f32[32,2048]{1,0:T(8,128)S(1)} %get-tuple-element.110.field_ref.refs_3_.refs_4_, bf16[896,2048]{1,0:T(8,128)(2,1)S(1)} %get-tuple-element.89.high_ref.refs_1_, bf16[896,2048]{1,0:T(8,128)(2,1)S(1)} %copy-done.1), custom_call_target="tpu_custom_call" | custom-call | flops 3000000000 | bytes 1048576 | tf_op jit(solution)/shard_map/pallas_call | solution.py:78
  64.8 2.9 %shard_map.80.refs_8_ = f32[32,2048]{1,0:T(8,128)S(1)} custom-call(s32[1]{0:T(128)} %bitcast.place_ref.refs_0_, s32[4,3]{1,0:T(4,128)S(1)} %copy-done.6, f32[32,2048]{1,0:T(8,128)S(1)} %get-tuple-element.110.field_ref.refs_3_.refs_4_, f32[1,2048]{1,0:T(1,128)S(1)} %bitcast.6, bf16[7,512,512]{2,1,0:T(8,128)(2,1)S(1)} %get-tuple-element.95.high_ref, ...), custom_call_target="tpu_custom_call" | custom-call | flops 3000000000 | bytes 1048576 | tf_op jit(solution)/shard_map/pallas_call | solution.py:78
  67.8 1.5 shard_map.82
  69.2 4.6 %collective-permute-start.10 = (f32[168,128]{1,0:T(8,128)S(1)}, f32[168,128]{1,0:T(8,128)S(1)}, u32[]{:S(2)}, u32[]{:S(2)}) collective-permute-start(f32[168,128]{1,0:T(8,128)S(1)} %get-tuple-element.119.refs_0_), channel_id=1, source_target_pairs={{0,1},{2,3},{4,5},{6,7},{8,9},{10,11},{12,13},{14,15},{16,17},{18,... | collective-permute-start | bytes 258056 | tf_op jit(solution)/shard_map/ppermute | solution.py:341
  79.9 18.5 %collective-permute-done.15.refs_6_ = f32[168,128]{1,0:T(8,128)S(1)} collective-permute-done((f32[168,128]{1,0:T(8,128)S(1)}, f32[168,128]{1,0:T(8,128)S(1)}, u32[]{:S(2)}, u32[]{:S(2)}) %collective-permute-start.15) | collective-permute-done | bytes 86048 | tf_op jit(solution)/shard_map/ppermute | solution.py:341
  100.9 2.3 %shard_map.90 = (f32[32,384]{1,0:T(8,128)S(1)}, f32[160,128]{1,0:T(8,128)S(1)}) custom-call(f32[32,2048]{1,0:T(8,128)S(1)} %get-tuple-element.132.field_ref.refs_3_.refs_4_, bf16[896,2048]{1,0:T(8,128)(2,1)S(1)} %get-tuple-element.89.high_ref.refs_1_, bf16[896,2048]{1,0:T(8,128)(2,1)S(1)} %copy-done.1), custom_call_target="tpu_custom_call" | custom-call | flops 3000000000 | bytes 1048576 | tf_op jit(solution)/shard_map/pallas_call | solution.py:78
  103.2 2.9 %shard_map.89.refs_8_ = f32[32,2048]{1,0:T(8,128)S(1)} custom-call(s32[1]{0:T(128)} %bitcast.place_ref.refs_0_, s32[4,3]{1,0:T(4,128)S(1)} %copy-done.6, f32[32,2048]{1,0:T(8,128)S(1)} %get-tuple-element.132.field_ref.refs_3_.refs_4_, f32[1,2048]{1,0:T(1,128)S(1)} %bitcast.7, bf16[7,512,512]{2,1,0:T(8,128)(2,1)S(1)} %get-tuple-element.95.high_ref, ...), custom_call_target="tpu_custom_call" | custom-call | flops 3000000000 | bytes 1048576 | tf_op jit(solution)/shard_map/pallas_call | solution.py:78
  106.1 1.5 shard_map.91
  107.6 4.8 %collective-permute-start.18 = (f32[168,128]{1,0:T(8,128)S(1)}, f32[168,128]{1,0:T(8,128)S(1)}, u32[]{:S(2)}, u32[]{:S(2)}) collective-permute-start(f32[168,128]{1,0:T(8,128)S(1)} %get-tuple-element.141.refs_0_), channel_id=1, source_target_pairs={{0,1},{2,3},{4,5},{6,7},{8,9},{10,11},{12,13},{14,15},{16,17},{18,... | collective-permute-start | bytes 258056 | tf_op jit(solution)/shard_map/ppermute | solution.py:341
  118.5 18.6 %collective-permute-done.23.refs_6_ = f32[168,128]{1,0:T(8,128)S(1)} collective-permute-done((f32[168,128]{1,0:T(8,128)S(1)}, f32[168,128]{1,0:T(8,128)S(1)}, u32[]{:S(2)}, u32[]{:S(2)}) %collective-permute-start.23) | collective-permute-done | bytes 86048 | tf_op jit(solution)/shard_map/ppermute | solution.py:341
  138.6 2.9 %shard_map.98.refs_8_ = f32[32,2048]{1,0:T(8,128)S(1)} custom-call(s32[1]{0:T(128)} %bitcast.place_ref.refs_0_, s32[4,3]{1,0:T(4,128)S(1)} %copy-done.6, f32[32,2048]{1,0:T(8,128)S(1)} %get-tuple-element.154.field_ref.refs_3_.refs_4_, f32[1,2048]{1,0:T(1,128)S(1)} %bitcast.8, bf16[7,512,512]{2,1,0:T(8,128)(2,1)S(1)} %get-tuple-element.95.high_ref, ...), custom_call_target="tpu_custom_call" | custom-call | flops 3000000000 | bytes 1048576 | tf_op jit(solution)/shard_map/pallas_call | solution.py:78
  142.3 2.3 %shard_map.99 = (f32[32,384]{1,0:T(8,128)S(1)}, f32[160,128]{1,0:T(8,128)S(1)}) custom-call(f32[32,2048]{1,0:T(8,128)S(1)} %get-tuple-element.154.field_ref.refs_3_.refs_4_, bf16[896,2048]{1,0:T(8,128)(2,1)S(1)} %get-tuple-element.89.high_ref.refs_1_, bf16[896,2048]{1,0:T(8,128)(2,1)S(1)} %copy-done.1), custom_call_target="tpu_custom_call" | custom-call | flops 3000000000 | bytes 1048576 | tf_op jit(solution)/shard_map/pallas_call | solution.py:78
  144.7 1.5 shard_map.100
  146.1 5.1 %collective-permute-start.26 = (f32[168,128]{1,0:T(8,128)S(1)}, f32[168,128]{1,0:T(8,128)S(1)}, u32[]{:S(2)}, u32[]{:S(2)}) collective-permute-start(f32[168,128]{1,0:T(8,128)S(1)} %get-tuple-element.163.refs_0_), channel_id=1, source_target_pairs={{0,1},{2,3},{4,5},{6,7},{8,9},{10,11},{12,13},{14,15},{16,17},{18,... | collective-permute-start | bytes 258056 | tf_op jit(solution)/shard_map/ppermute | solution.py:341
  157.4 19.4 %collective-permute-done.31.refs_6_ = f32[168,128]{1,0:T(8,128)S(1)} collective-permute-done((f32[168,128]{1,0:T(8,128)S(1)}, f32[168,128]{1,0:T(8,128)S(1)}, u32[]{:S(2)}, u32[]{:S(2)}) %collective-permute-start.31) | collective-permute-done | bytes 86048 | tf_op jit(solution)/shard_map/ppermute | solution.py:341
  176.8 2.2 %shard_map.106 = (f32[32,2048]{1,0:T(8,128)}, f32[32,2048]{1,0:T(8,128)}) custom-call(s32[1]{0:T(128)S(6)} %select_n.7.core_ref.refs_1_.refs_0_, bf16[896,2048]{1,0:T(8,128)(2,1)S(1)} %get-tuple-element.89.high_ref.refs_1_, bf16[896,2048]{1,0:T(8,128)(2,1)S(1)} %copy-done.1, f32[32,2048]{1,0:T(8,128)S(1)} %get-tuple-element.162.refs_3_, ...), custom_call_target="tpu_custom_call" | custom-call | flops 1500000000 | bytes 1048576 | tf_op jit(solution)/shard_map/pallas_call | solution.py:78
  (96 shorter events, 36.1 us)
Async XLA Ops:
  2.4 23.2 %collective-permute-start = (f32[40,512]{1,0:T(8,128)S(1)}, f32[40,512]{1,0:T(8,128)S(1)}, u32[]{:S(2)}, u32[]{:S(2)}) collective-permute-start(f32[40,512]{1,0:T(8,128)S(1)} %get-tuple-element.91), channel_id=1, source_target_pairs={{0,1},{1,0},{2,3},{3,2},{4,5},{5,4},{6,7},{7,6},{8,9},{9,8},{10,11... | collective-permute-start | bytes 245768 | tf_op jit(solution)/shard_map/ppermute | solution.py:341
  2.9 22.7 %collective-permute-start.1 = (f32[40,512]{1,0:T(8,128)S(1)}, f32[40,512]{1,0:T(8,128)S(1)}, u32[]{:S(2)}, u32[]{:S(2)}) collective-permute-start(f32[40,512]{1,0:T(8,128)S(1)} %get-tuple-element.92), channel_id=1, source_target_pairs={{1,2},{3,4},{5,6},{7,8},{9,10},{11,12},{13,14},{15,16},{17,18},{19... | collective-permute-start | bytes 245768 | tf_op jit(solution)/shard_map/ppermute | solution.py:341
  29.7 6.7 %collective-permute-start.2 = (f32[168,128]{1,0:T(8,128)S(1)}, f32[168,128]{1,0:T(8,128)S(1)}, u32[]{:S(2)}, u32[]{:S(2)}) collective-permute-start(f32[168,128]{1,0:T(8,128)S(1)} %get-tuple-element.100.refs_0_), channel_id=1, source_target_pairs={{0,1},{2,3},{4,5},{6,7},{8,9},{10,11},{12,13},{14,15},{16,17},{18,... | collective-permute-start | bytes 258056 | tf_op jit(solution)/shard_map/ppermute | solution.py:341
  36.6 0.7 collective-permute-start.3
  37.4 0.7 collective-permute-start.4
  38.2 0.7 collective-permute-start.5
  40.3 19.9 %collective-permute-start.7 = (f32[168,128]{1,0:T(8,128)S(1)}, f32[168,128]{1,0:T(8,128)S(1)}, u32[]{:S(2)}, u32[]{:S(2)}) collective-permute-start(f32[168,128]{1,0:T(8,128)S(1)} %get-tuple-element.109.refs_5_), channel_id=1, source_target_pairs={{1,0},{3,2},{5,4},{7,6},{9,8},{11,10},{13,12},{15,14},{17,16},{19,... | collective-permute-start | bytes 258056 | tf_op jit(solution)/shard_map/ppermute | solution.py:341
  61.6 6.1 %collective-permute-start.8 = (f32[32,512]{1,0:T(8,128)S(1)}, f32[32,512]{1,0:T(8,128)S(1)}, u32[]{:S(2)}, u32[]{:S(2)}) collective-permute-start(f32[32,512]{1,0:T(8,128)S(1)} %get-tuple-element.111), channel_id=1, source_target_pairs={{0,1},{1,0},{2,3},{3,2},{4,5},{5,4},{6,7},{7,6},{8,9},{9,8},{10,11... | collective-permute-start | bytes 196616 | tf_op jit(solution)/shard_map/ppermute | solution.py:341
  61.9 5.9 %collective-permute-start.9 = (f32[32,512]{1,0:T(8,128)S(1)}, f32[32,512]{1,0:T(8,128)S(1)}, u32[]{:S(2)}, u32[]{:S(2)}) collective-permute-start(f32[32,512]{1,0:T(8,128)S(1)} %get-tuple-element.112), channel_id=1, source_target_pairs={{1,2},{3,4},{5,6},{7,8},{9,10},{11,12},{13,14},{15,16},{17,18},{19... | collective-permute-start | bytes 196616 | tf_op jit(solution)/shard_map/ppermute | solution.py:341
  69.2 5.5 %collective-permute-start.10 = (f32[168,128]{1,0:T(8,128)S(1)}, f32[168,128]{1,0:T(8,128)S(1)}, u32[]{:S(2)}, u32[]{:S(2)}) collective-permute-start(f32[168,128]{1,0:T(8,128)S(1)} %get-tuple-element.119.refs_0_), channel_id=1, source_target_pairs={{0,1},{2,3},{4,5},{6,7},{8,9},{10,11},{12,13},{14,15},{16,17},{18,... | collective-permute-start | bytes 258056 | tf_op jit(solution)/shard_map/ppermute | solution.py:341
  76.5 0.7 collective-permute-start.13
  77.4 0.7 collective-permute-start.14
  78.6 19.7 %collective-permute-start.15 = (f32[168,128]{1,0:T(8,128)S(1)}, f32[168,128]{1,0:T(8,128)S(1)}, u32[]{:S(2)}, u32[]{:S(2)}) collective-permute-start(f32[168,128]{1,0:T(8,128)S(1)} %get-tuple-element.129.refs_5_), channel_id=1, source_target_pairs={{1,0},{3,2},{5,4},{7,6},{9,8},{11,10},{13,12},{15,14},{17,16},{19,... | collective-permute-start | bytes 258056 | tf_op jit(solution)/shard_map/ppermute | solution.py:341
  99.9 6.3 %collective-permute-start.16 = (f32[32,512]{1,0:T(8,128)S(1)}, f32[32,512]{1,0:T(8,128)S(1)}, u32[]{:S(2)}, u32[]{:S(2)}) collective-permute-start(f32[32,512]{1,0:T(8,128)S(1)} %get-tuple-element.133), channel_id=1, source_target_pairs={{0,1},{1,0},{2,3},{3,2},{4,5},{5,4},{6,7},{7,6},{8,9},{9,8},{10,11... | collective-permute-start | bytes 196616 | tf_op jit(solution)/shard_map/ppermute | solution.py:341
  100.1 6.1 %collective-permute-start.17 = (f32[32,512]{1,0:T(8,128)S(1)}, f32[32,512]{1,0:T(8,128)S(1)}, u32[]{:S(2)}, u32[]{:S(2)}) collective-permute-start(f32[32,512]{1,0:T(8,128)S(1)} %get-tuple-element.134), channel_id=1, source_target_pairs={{1,2},{3,4},{5,6},{7,8},{9,10},{11,12},{13,14},{15,16},{17,18},{19... | collective-permute-start | bytes 196616 | tf_op jit(solution)/shard_map/ppermute | solution.py:341
  107.6 5.7 %collective-permute-start.18 = (f32[168,128]{1,0:T(8,128)S(1)}, f32[168,128]{1,0:T(8,128)S(1)}, u32[]{:S(2)}, u32[]{:S(2)}) collective-permute-start(f32[168,128]{1,0:T(8,128)S(1)} %get-tuple-element.141.refs_0_), channel_id=1, source_target_pairs={{0,1},{2,3},{4,5},{6,7},{8,9},{10,11},{12,13},{14,15},{16,17},{18,... | collective-permute-start | bytes 258056 | tf_op jit(solution)/shard_map/ppermute | solution.py:341
  115.1 0.7 collective-permute-start.21
  115.9 0.7 collective-permute-start.22
  117.2 19.9 %collective-permute-start.23 = (f32[168,128]{1,0:T(8,128)S(1)}, f32[168,128]{1,0:T(8,128)S(1)}, u32[]{:S(2)}, u32[]{:S(2)}) collective-permute-start(f32[168,128]{1,0:T(8,128)S(1)} %get-tuple-element.151.refs_5_), channel_id=1, source_target_pairs={{1,0},{3,2},{5,4},{7,6},{9,8},{11,10},{13,12},{15,14},{17,16},{19,... | collective-permute-start | bytes 258056 | tf_op jit(solution)/shard_map/ppermute | solution.py:341
  141.5 3.2 %collective-permute-start.24 = (f32[32,512]{1,0:T(8,128)S(1)}, f32[32,512]{1,0:T(8,128)S(1)}, u32[]{:S(2)}, u32[]{:S(2)}) collective-permute-start(f32[32,512]{1,0:T(8,128)S(1)} %get-tuple-element.155), channel_id=1, source_target_pairs={{0,1},{1,0},{2,3},{3,2},{4,5},{5,4},{6,7},{7,6},{8,9},{9,8},{10,11... | collective-permute-start | bytes 196616 | tf_op jit(solution)/shard_map/ppermute | solution.py:341
  141.7 3.0 %collective-permute-start.25 = (f32[32,512]{1,0:T(8,128)S(1)}, f32[32,512]{1,0:T(8,128)S(1)}, u32[]{:S(2)}, u32[]{:S(2)}) collective-permute-start(f32[32,512]{1,0:T(8,128)S(1)} %get-tuple-element.156), channel_id=1, source_target_pairs={{1,2},{3,4},{5,6},{7,8},{9,10},{11,12},{13,14},{15,16},{17,18},{19... | collective-permute-start | bytes 196616 | tf_op jit(solution)/shard_map/ppermute | solution.py:341
  146.1 6.1 %collective-permute-start.26 = (f32[168,128]{1,0:T(8,128)S(1)}, f32[168,128]{1,0:T(8,128)S(1)}, u32[]{:S(2)}, u32[]{:S(2)}) collective-permute-start(f32[168,128]{1,0:T(8,128)S(1)} %get-tuple-element.163.refs_0_), channel_id=1, source_target_pairs={{0,1},{2,3},{4,5},{6,7},{8,9},{10,11},{12,13},{14,15},{16,17},{18,... | collective-permute-start | bytes 258056 | tf_op jit(solution)/shard_map/ppermute | solution.py:341
  154.8 0.7 collective-permute-start.30
  156.1 20.7 %collective-permute-start.31 = (f32[168,128]{1,0:T(8,128)S(1)}, f32[168,128]{1,0:T(8,128)S(1)}, u32[]{:S(2)}, u32[]{:S(2)}) collective-permute-start(f32[168,128]{1,0:T(8,128)S(1)} %get-tuple-element.173.refs_5_), channel_id=1, source_target_pairs={{1,0},{3,2},{5,4},{7,6},{9,8},{11,10},{13,12},{15,14},{17,16},{19,... | collective-permute-start | bytes 258056 | tf_op jit(solution)/shard_map/ppermute | solution.py:341
  (16 other events, 62.0 us)
where the time goes:
time: 180 us; the launch traced here: 179 us
  waiting for transfers between devices  78.7 us (44%)
  Pallas kernels  53.5 us (30%)
  starting transfers between devices  39.9 us (22%)
  local copies, waits for them, and re-layouts  5.63 us (3%)
    ppermute x32, waiting for transfers between devices, send(): return lax.ppermute(value, BOTH, pairs)  78.7 us
    pallas_call x38, Pallas kernels, call(): pl.pallas_call(body, out_shape=outs, in_specs=[whole(pltpu.SMEM)] * scala...  40.7 us
    ppermute x32, starting transfers between devices, send(): return lax.ppermute(value, BOTH, pairs)  39.9 us
    pallas_call x1, Pallas kernels, per_device(): pl.pallas_call(setup_kernel, out_shape=[bf16(2 * leaves - 1, LEAF, LEAF)]...  12.8 us
    unnamed x17, local copies, waits for them, and re-layouts  5.63 us
  transfers between devices with their start and end apart: 32, of which 8 were waited for; matrix products, arithmetic and copies ran while one was open for 1% of the time, Pallas kernels for 17%

commit v1 on v0

--- a/solution.py
+++ b/solution.py
@@ -74,7 +74,7 @@
     return pl.BlockSpec(memory_space=memory)
 
 
-def call(body, outs, *args, scalars=0, flops=0, limit=32):
+def call(body, outs, *args, scalars=0, flops=0, limit=16):
     return pl.pallas_call(
         body,
         out_shape=outs,
@@ -188,7 +188,7 @@
     found = ids_ref[leaf, 0] == target
     for slot in range(1, WIN):
         found = jnp.logical_or(found, ids_ref[leaf, slot] == target)
-    return jnp.where(found, 1.0 / (16 * WIN), 0.0)
+    return jnp.where(jnp.logical_and(found, target >= 0), 1.0 / (16 * WIN), 0.0)
 
 
 def inner_kernel(place_ref, ids_ref, field_ref, nugget_ref, high_ref, low_ref, out_ref):
@@ -336,14 +336,15 @@
     core = place % 2
 
     even = range(0, devices, 2)
+    inside = [(index, index ^ 1) for index in range(devices)]
 
     def send(value, pairs):
         return lax.ppermute(value, BOTH, pairs)
 
     def halo(paired, other):
         outward = [(index, index + 1) for index in range(1, devices - 1, 2)]
-        inside = [(index, index ^ 1) for index in range(devices)]
-        return send(paired, inside), send(other, outward + [(target, source) for source, target in outward])
+        ends = [(0, 0), (devices - 1, devices - 1)]
+        return send(paired, inside), send(other, outward + [(target, source) for source, target in outward] + ends)
 
     edges = call(edges_kernel, [f32(rows + TILE, LEAF)] * 2, core, rhs, coords, scalars=1)
     edges = halo(*edges)
@@ -354,7 +355,7 @@
         in_specs=[whole(), whole(), whole(pltpu.HBM)],
         out_specs=[whole()] * 4,
         scratch_shapes=[pltpu.VMEM(basis.shape, jnp.float32), pltpu.SemaphoreType.DMA((levels,))],
-        compiler_params=pltpu.CompilerParams(vmem_limit_bytes=40 * 2**20),
+        compiler_params=pltpu.CompilerParams(vmem_limit_bytes=24 * 2**20),
         cost_estimate=pl.CostEstimate(flops=4 * FLOPS, bytes_accessed=2**20, transcendentals=0),
     )(coords, turned, basis)
     edge_pair = call(
@@ -395,9 +396,10 @@
         for bit in range(crossing):
             left = crossing - bit - 1
             if bit == 0:
-                got = send(message, [(index, index + 1) for index in even])
+                got = send(message, inside)
             else:
-                got = send(message, [(index + 1, (index + 1) ^ (1 << bit)) for index in even])
+                outside = [(index + 1, (index + 1) ^ (1 << bit)) for index in even]
+                got = send(message, outside + [(index, index) for index in even])
             args = [message, got] + ([] if first else [carried[3]]) + (done if left == 0 else [])
             message, level = call(
                 functools.partial(combine_kernel, first, bit, width * (2 << bit)),
@@ -405,7 +407,7 @@
                 *args,
             )
             done.append(level)
-        got = send(message, [(index + 1, index) for index in even])
+        got = send(message, inside)
         args = [core, high, low, near, field, message, got, local]
         if not first:
             args = args + [solution, *carried]

time: 180 us -> 170 us (0.944)
  waiting for transfers between devices: 78.7 us -> 7.5 us
  starting transfers between devices: 39.9 us -> 101 us
    ppermute x32, waiting for transfers between devices: 78.7 us -> 7.5 us  [send(): return lax.ppermute(value, BOTH, pairs)]
    ppermute x32, starting transfers between devices: 39.9 us -> 101 us  [send(): return lax.ppermute(value, BOTH, pairs)]
    unnamed x17 -> x15, local copies, waits for them, and re-layouts: 5.63 us -> 6.68 us
where the time goes in v1:
time: 170 us; the launch traced here: 169 us
  starting transfers between devices  101 us (59%)
  Pallas kernels  52.2 us (31%)
  waiting for transfers between devices  7.5 us (4%)
  local copies, waits for them, and re-layouts  6.68 us (4%)
    ppermute x32, starting transfers between devices, send(): return lax.ppermute(value, BOTH, pairs)  101 us
    pallas_call x38, Pallas kernels, call(): pl.pallas_call(body, out_shape=outs, in_specs=[whole(pltpu.SMEM)] * scala...  40.7 us
    pallas_call x1, Pallas kernels, per_device(): pl.pallas_call(setup_kernel, out_shape=[bf16(2 * leaves - 1, LEAF, LEAF)]...  11.6 us
    ppermute x32, waiting for transfers between devices, send(): return lax.ppermute(value, BOTH, pairs)  7.5 us
    unnamed x15, local copies, waits for them, and re-layouts  6.68 us
  transfers between devices with their start and end apart: 32, of which 8 were waited for; matrix products, arithmetic and copies ran while one was open for 1% of the time, Pallas kernels for 17%

profile of v1, /device:TPU:0, one launch (start us, length us, event | category | flops | bytes accessed | tf_op | source)
XLA Modules:
  0.0 169.0 jit_solution(9832137056358229604)
XLA Ops:
  5.4 3.1 %copy-done.5 = f32[7,128,2048]{2,1,0:T(8,128)S(1)} copy-done((f32[7,128,2048]{2,1,0:T(8,128)S(1)}, f32[7,128,2048]{2,1,0:T(8,128)}, u32[]{:S(2)}) %copy-start.5) | copy-done | bytes 7340056
  8.5 11.6 %shard_map.68 = (bf16[7,512,512]{2,1,0:T(8,128)(2,1)S(1)}, bf16[7,512,512]{2,1,0:T(8,128)(2,1)S(1)}, bf16[896,2048]{1,0:T(8,128)(2,1)S(1)}, bf16[896,2048]{1,0:T(8,128)(2,1)S(1)}) custom-call(f32[3,2048]{1,0:T(4,128)S(1)} %copy-done.3, f32[2048,3]{1,0:T(8,128)S(1)} %bitcast.3, f32[7,128,2048]{2,1,0:T(8,128)S(1)} %copy-done.5), custom_call_target="tpu_custom_call" | custom-call | flops 12000000000 | bytes 1048576 | tf_op jit(solution)/shard_map/pallas_call | solution.py:352
  20.1 2.3 %shard_map.72 = (f32[32,384]{1,0:T(8,128)S(1)}, f32[160,128]{1,0:T(8,128)S(1)}) custom-call(f32[32,2048]{1,0:T(8,128)S(1)} %copy-done.1, bf16[896,2048]{1,0:T(8,128)(2,1)S(1)} %get-tuple-element.89.high_ref.refs_1_, bf16[896,2048]{1,0:T(8,128)(2,1)S(1)} %get-tuple-element.90.low_ref.refs_2_), custom_call_target="tpu_custom_call" | custom-call | flops 3000000000 | bytes 1048576 | tf_op jit(solution)/shard_map/pallas_call | solution.py:78
  22.5 2.9 %shard_map.71.refs_8_ = f32[32,2048]{1,0:T(8,128)S(1)} custom-call(s32[1]{0:T(128)} %bitcast.place_ref.refs_0_, s32[4,3]{1,0:T(4,128)S(1)} %copy-done.4, f32[32,2048]{1,0:T(8,128)S(1)} %copy-done.1, f32[1,2048]{1,0:T(1,128)S(1)} %bitcast.5, bf16[7,512,512]{2,1,0:T(8,128)(2,1)S(1)} %get-tuple-element.95.high_ref, ...), custom_call_target="tpu_custom_call" | custom-call | flops 3000000000 | bytes 1048576 | tf_op jit(solution)/shard_map/pallas_call | solution.py:78
  25.3 2.7 %shard_map.70 = (bf16[2,512,512]{2,1,0:T(8,128)(2,1)S(1)}, bf16[2,512,512]{2,1,0:T(8,128)(2,1)S(1)}) custom-call(s32[1]{0:T(128)S(6)} %select_n.7.core_ref.refs_1_.refs_0_, f32[2048,3]{1,0:T(8,128)S(1)} %bitcast.4, f32[40,512]{1,0:T(8,128)S(1)} %collective-permute-done.refs_1_.refs_4_, f32[40,512]{1,0:T(8,128)S(1)} %collective-permute-done.1.refs_2_.refs_5_), custom_call_target="tpu_custom_call" | custom-call | flops 3000000000 | bytes 1048576 | tf_op jit(solution)/shard_map/pallas_call | solution.py:78
  28.0 1.5 shard_map.73
  29.5 3.9 %collective-permute-start.2 = (f32[168,128]{1,0:T(8,128)S(1)}, f32[168,128]{1,0:T(8,128)S(1)}, u32[]{:S(2)}, u32[]{:S(2)}) collective-permute-start(f32[168,128]{1,0:T(8,128)S(1)} %get-tuple-element.100.refs_0_), channel_id=1, source_target_pairs={{0,1},{1,0},{2,3},{3,2},{4,5},{5,4},{6,7},{7,6},{8,9},{9,8},{10,11... | collective-permute-start | bytes 258056 | tf_op jit(solution)/shard_map/ppermute | solution.py:342
  38.2 18.6 %collective-permute-start.7 = (f32[168,128]{1,0:T(8,128)S(1)}, f32[168,128]{1,0:T(8,128)S(1)}, u32[]{:S(2)}, u32[]{:S(2)}) collective-permute-start(f32[168,128]{1,0:T(8,128)S(1)} %get-tuple-element.109.refs_5_), channel_id=1, source_target_pairs={{0,1},{1,0},{2,3},{3,2},{4,5},{5,4},{6,7},{7,6},{8,9},{9,8},{10,11... | collective-permute-start | bytes 258056 | tf_op jit(solution)/shard_map/ppermute | solution.py:342
  60.3 2.3 %shard_map.81 = (f32[32,384]{1,0:T(8,128)S(1)}, f32[160,128]{1,0:T(8,128)S(1)}) custom-call(f32[32,2048]{1,0:T(8,128)S(1)} %get-tuple-element.110.field_ref.refs_3_.refs_4_, bf16[896,2048]{1,0:T(8,128)(2,1)S(1)} %get-tuple-element.89.high_ref.refs_1_, bf16[896,2048]{1,0:T(8,128)(2,1)S(1)} %get-tuple-element.90.low_ref.refs_2_), custom_call_target="tpu_custom_call" | custom-call | flops 3000000000 | bytes 1048576 | tf_op jit(solution)/shard_map/pallas_call | solution.py:78
  62.6 2.9 %shard_map.80.refs_8_ = f32[32,2048]{1,0:T(8,128)S(1)} custom-call(s32[1]{0:T(128)} %bitcast.place_ref.refs_0_, s32[4,3]{1,0:T(4,128)S(1)} %copy-done.4, f32[32,2048]{1,0:T(8,128)S(1)} %get-tuple-element.110.field_ref.refs_3_.refs_4_, f32[1,2048]{1,0:T(1,128)S(1)} %bitcast.6, bf16[7,512,512]{2,1,0:T(8,128)(2,1)S(1)} %get-tuple-element.95.high_ref, ...), custom_call_target="tpu_custom_call" | custom-call | flops 3000000000 | bytes 1048576 | tf_op jit(solution)/shard_map/pallas_call | solution.py:78
  67.0 1.9 %collective-permute-start.10 = (f32[168,128]{1,0:T(8,128)S(1)}, f32[168,128]{1,0:T(8,128)S(1)}, u32[]{:S(2)}, u32[]{:S(2)}) collective-permute-start(f32[168,128]{1,0:T(8,128)S(1)} %get-tuple-element.119.refs_0_), channel_id=1, source_target_pairs={{0,1},{1,0},{2,3},{3,2},{4,5},{5,4},{6,7},{7,6},{8,9},{9,8},{10,11... | collective-permute-start | bytes 258056 | tf_op jit(solution)/shard_map/ppermute | solution.py:342
  73.7 18.3 %collective-permute-start.15 = (f32[168,128]{1,0:T(8,128)S(1)}, f32[168,128]{1,0:T(8,128)S(1)}, u32[]{:S(2)}, u32[]{:S(2)}) collective-permute-start(f32[168,128]{1,0:T(8,128)S(1)} %get-tuple-element.129.refs_5_), channel_id=1, source_target_pairs={{0,1},{1,0},{2,3},{3,2},{4,5},{5,4},{6,7},{7,6},{8,9},{9,8},{10,11... | collective-permute-start | bytes 258056 | tf_op jit(solution)/shard_map/ppermute | solution.py:342
  95.7 2.3 %shard_map.90 = (f32[32,384]{1,0:T(8,128)S(1)}, f32[160,128]{1,0:T(8,128)S(1)}) custom-call(f32[32,2048]{1,0:T(8,128)S(1)} %get-tuple-element.132.field_ref.refs_3_.refs_4_, bf16[896,2048]{1,0:T(8,128)(2,1)S(1)} %get-tuple-element.89.high_ref.refs_1_, bf16[896,2048]{1,0:T(8,128)(2,1)S(1)} %get-tuple-element.90.low_ref.refs_2_), custom_call_target="tpu_custom_call" | custom-call | flops 3000000000 | bytes 1048576 | tf_op jit(solution)/shard_map/pallas_call | solution.py:78
  98.0 2.9 %shard_map.89.refs_8_ = f32[32,2048]{1,0:T(8,128)S(1)} custom-call(s32[1]{0:T(128)} %bitcast.place_ref.refs_0_, s32[4,3]{1,0:T(4,128)S(1)} %copy-done.4, f32[32,2048]{1,0:T(8,128)S(1)} %get-tuple-element.132.field_ref.refs_3_.refs_4_, f32[1,2048]{1,0:T(1,128)S(1)} %bitcast.7, bf16[7,512,512]{2,1,0:T(8,128)(2,1)S(1)} %get-tuple-element.95.high_ref, ...), custom_call_target="tpu_custom_call" | custom-call | flops 3000000000 | bytes 1048576 | tf_op jit(solution)/shard_map/pallas_call | solution.py:78
  100.9 1.5 shard_map.91
  102.4 3.1 %collective-permute-start.18 = (f32[168,128]{1,0:T(8,128)S(1)}, f32[168,128]{1,0:T(8,128)S(1)}, u32[]{:S(2)}, u32[]{:S(2)}) collective-permute-start(f32[168,128]{1,0:T(8,128)S(1)} %get-tuple-element.141.refs_0_), channel_id=1, source_target_pairs={{0,1},{1,0},{2,3},{3,2},{4,5},{5,4},{6,7},{7,6},{8,9},{9,8},{10,11... | collective-permute-start | bytes 258056 | tf_op jit(solution)/shard_map/ppermute | solution.py:342
  110.3 18.4 %collective-permute-start.23 = (f32[168,128]{1,0:T(8,128)S(1)}, f32[168,128]{1,0:T(8,128)S(1)}, u32[]{:S(2)}, u32[]{:S(2)}) collective-permute-start(f32[168,128]{1,0:T(8,128)S(1)} %get-tuple-element.151.refs_5_), channel_id=1, source_target_pairs={{0,1},{1,0},{2,3},{3,2},{4,5},{5,4},{6,7},{7,6},{8,9},{9,8},{10,11... | collective-permute-start | bytes 258056 | tf_op jit(solution)/shard_map/ppermute | solution.py:342
  129.7 1.5 shard_map.97
  131.1 2.9 %shard_map.98.refs_8_ = f32[32,2048]{1,0:T(8,128)S(1)} custom-call(s32[1]{0:T(128)} %bitcast.place_ref.refs_0_, s32[4,3]{1,0:T(4,128)S(1)} %copy-done.4, f32[32,2048]{1,0:T(8,128)S(1)} %get-tuple-element.154.field_ref.refs_3_.refs_4_, f32[1,2048]{1,0:T(1,128)S(1)} %bitcast.8, bf16[7,512,512]{2,1,0:T(8,128)(2,1)S(1)} %get-tuple-element.95.high_ref, ...), custom_call_target="tpu_custom_call" | custom-call | flops 3000000000 | bytes 1048576 | tf_op jit(solution)/shard_map/pallas_call | solution.py:78
  135.1 2.3 %shard_map.99 = (f32[32,384]{1,0:T(8,128)S(1)}, f32[160,128]{1,0:T(8,128)S(1)}) custom-call(f32[32,2048]{1,0:T(8,128)S(1)} %get-tuple-element.154.field_ref.refs_3_.refs_4_, bf16[896,2048]{1,0:T(8,128)(2,1)S(1)} %get-tuple-element.89.high_ref.refs_1_, bf16[896,2048]{1,0:T(8,128)(2,1)S(1)} %get-tuple-element.90.low_ref.refs_2_), custom_call_target="tpu_custom_call" | custom-call | flops 3000000000 | bytes 1048576 | tf_op jit(solution)/shard_map/pallas_call | solution.py:78
  137.4 1.5 shard_map.100
  138.9 3.3 %collective-permute-start.26 = (f32[168,128]{1,0:T(8,128)S(1)}, f32[168,128]{1,0:T(8,128)S(1)}, u32[]{:S(2)}, u32[]{:S(2)}) collective-permute-start(f32[168,128]{1,0:T(8,128)S(1)} %get-tuple-element.163.refs_0_), channel_id=1, source_target_pairs={{0,1},{1,0},{2,3},{3,2},{4,5},{5,4},{6,7},{7,6},{8,9},{9,8},{10,11... | collective-permute-start | bytes 258056 | tf_op jit(solution)/shard_map/ppermute | solution.py:342
  147.1 18.9 %collective-permute-start.31 = (f32[168,128]{1,0:T(8,128)S(1)}, f32[168,128]{1,0:T(8,128)S(1)}, u32[]{:S(2)}, u32[]{:S(2)}) collective-permute-start(f32[168,128]{1,0:T(8,128)S(1)} %get-tuple-element.173.refs_5_), channel_id=1, source_target_pairs={{0,1},{1,0},{2,3},{3,2},{4,5},{5,4},{6,7},{7,6},{8,9},{9,8},{10,11... | collective-permute-start | bytes 258056 | tf_op jit(solution)/shard_map/ppermute | solution.py:342
  166.9 2.2 %shard_map.106 = (f32[32,2048]{1,0:T(8,128)}, f32[32,2048]{1,0:T(8,128)}) custom-call(s32[1]{0:T(128)S(6)} %select_n.7.core_ref.refs_1_.refs_0_, bf16[896,2048]{1,0:T(8,128)(2,1)S(1)} %get-tuple-element.89.high_ref.refs_1_, bf16[896,2048]{1,0:T(8,128)(2,1)S(1)} %get-tuple-element.90.low_ref.refs_2_, f32[32,2048]{1,0:T(8,128)S(1)} %get-tuple-element.162.refs_3_, ...), custom_call_target="tpu_custom_call" | custom-call | flops 1500000000 | bytes 1048576 | tf_op jit(solution)/shard_map/pallas_call | solution.py:78
  (94 shorter events, 35.4 us)
Async XLA Ops:
  2.4 23.0 %collective-permute-start = (f32[40,512]{1,0:T(8,128)S(1)}, f32[40,512]{1,0:T(8,128)S(1)}, u32[]{:S(2)}, u32[]{:S(2)}) collective-permute-start(f32[40,512]{1,0:T(8,128)S(1)} %get-tuple-element.91), channel_id=1, source_target_pairs={{0,1},{1,0},{2,3},{3,2},{4,5},{5,4},{6,7},{7,6},{8,9},{9,8},{10,11... | collective-permute-start | bytes 245768 | tf_op jit(solution)/shard_map/ppermute | solution.py:342
  2.9 22.4 %collective-permute-start.1 = (f32[40,512]{1,0:T(8,128)S(1)}, f32[40,512]{1,0:T(8,128)S(1)}, u32[]{:S(2)}, u32[]{:S(2)}) collective-permute-start(f32[40,512]{1,0:T(8,128)S(1)} %get-tuple-element.92), channel_id=1, source_target_pairs={{1,2},{3,4},{5,6},{7,8},{9,10},{11,12},{13,14},{15,16},{17,18},{19... | collective-permute-start | bytes 245768 | tf_op jit(solution)/shard_map/ppermute | solution.py:342
  29.5 4.8 %collective-permute-start.2 = (f32[168,128]{1,0:T(8,128)S(1)}, f32[168,128]{1,0:T(8,128)S(1)}, u32[]{:S(2)}, u32[]{:S(2)}) collective-permute-start(f32[168,128]{1,0:T(8,128)S(1)} %get-tuple-element.100.refs_0_), channel_id=1, source_target_pairs={{0,1},{1,0},{2,3},{3,2},{4,5},{5,4},{6,7},{7,6},{8,9},{9,8},{10,11... | collective-permute-start | bytes 258056 | tf_op jit(solution)/shard_map/ppermute | solution.py:342
  34.5 0.7 collective-permute-start.3
  35.3 0.7 collective-permute-start.4
  36.1 0.7 collective-permute-start.5
  38.2 19.5 %collective-permute-start.7 = (f32[168,128]{1,0:T(8,128)S(1)}, f32[168,128]{1,0:T(8,128)S(1)}, u32[]{:S(2)}, u32[]{:S(2)}) collective-permute-start(f32[168,128]{1,0:T(8,128)S(1)} %get-tuple-element.109.refs_5_), channel_id=1, source_target_pairs={{0,1},{1,0},{2,3},{3,2},{4,5},{5,4},{6,7},{7,6},{8,9},{9,8},{10,11... | collective-permute-start | bytes 258056 | tf_op jit(solution)/shard_map/ppermute | solution.py:342
  59.2 6.3 %collective-permute-start.8 = (f32[32,512]{1,0:T(8,128)S(1)}, f32[32,512]{1,0:T(8,128)S(1)}, u32[]{:S(2)}, u32[]{:S(2)}) collective-permute-start(f32[32,512]{1,0:T(8,128)S(1)} %get-tuple-element.111), channel_id=1, source_target_pairs={{0,1},{1,0},{2,3},{3,2},{4,5},{5,4},{6,7},{7,6},{8,9},{9,8},{10,11... | collective-permute-start | bytes 196616 | tf_op jit(solution)/shard_map/ppermute | solution.py:342
  59.6 5.9 %collective-permute-start.9 = (f32[32,512]{1,0:T(8,128)S(1)}, f32[32,512]{1,0:T(8,128)S(1)}, u32[]{:S(2)}, u32[]{:S(2)}) collective-permute-start(f32[32,512]{1,0:T(8,128)S(1)} %get-tuple-element.112), channel_id=1, source_target_pairs={{1,2},{3,4},{5,6},{7,8},{9,10},{11,12},{13,14},{15,16},{17,18},{19... | collective-permute-start | bytes 196616 | tf_op jit(solution)/shard_map/ppermute | solution.py:342
  67.0 2.9 %collective-permute-start.10 = (f32[168,128]{1,0:T(8,128)S(1)}, f32[168,128]{1,0:T(8,128)S(1)}, u32[]{:S(2)}, u32[]{:S(2)}) collective-permute-start(f32[168,128]{1,0:T(8,128)S(1)} %get-tuple-element.119.refs_0_), channel_id=1, source_target_pairs={{0,1},{1,0},{2,3},{3,2},{4,5},{5,4},{6,7},{7,6},{8,9},{9,8},{10,11... | collective-permute-start | bytes 258056 | tf_op jit(solution)/shard_map/ppermute | solution.py:342
  71.6 0.7 collective-permute-start.13
  72.4 0.7 collective-permute-start.14
  73.7 19.2 %collective-permute-start.15 = (f32[168,128]{1,0:T(8,128)S(1)}, f32[168,128]{1,0:T(8,128)S(1)}, u32[]{:S(2)}, u32[]{:S(2)}) collective-permute-start(f32[168,128]{1,0:T(8,128)S(1)} %get-tuple-element.129.refs_5_), channel_id=1, source_target_pairs={{0,1},{1,0},{2,3},{3,2},{4,5},{5,4},{6,7},{7,6},{8,9},{9,8},{10,11... | collective-permute-start | bytes 258056 | tf_op jit(solution)/shard_map/ppermute | solution.py:342
  94.4 6.5 %collective-permute-start.16 = (f32[32,512]{1,0:T(8,128)S(1)}, f32[32,512]{1,0:T(8,128)S(1)}, u32[]{:S(2)}, u32[]{:S(2)}) collective-permute-start(f32[32,512]{1,0:T(8,128)S(1)} %get-tuple-element.133), channel_id=1, source_target_pairs={{0,1},{1,0},{2,3},{3,2},{4,5},{5,4},{6,7},{7,6},{8,9},{9,8},{10,11... | collective-permute-start | bytes 196616 | tf_op jit(solution)/shard_map/ppermute | solution.py:342
  94.8 6.1 %collective-permute-start.17 = (f32[32,512]{1,0:T(8,128)S(1)}, f32[32,512]{1,0:T(8,128)S(1)}, u32[]{:S(2)}, u32[]{:S(2)}) collective-permute-start(f32[32,512]{1,0:T(8,128)S(1)} %get-tuple-element.134), channel_id=1, source_target_pairs={{1,2},{3,4},{5,6},{7,8},{9,10},{11,12},{13,14},{15,16},{17,18},{19... | collective-permute-start | bytes 196616 | tf_op jit(solution)/shard_map/ppermute | solution.py:342
  102.4 4.0 %collective-permute-start.18 = (f32[168,128]{1,0:T(8,128)S(1)}, f32[168,128]{1,0:T(8,128)S(1)}, u32[]{:S(2)}, u32[]{:S(2)}) collective-permute-start(f32[168,128]{1,0:T(8,128)S(1)} %get-tuple-element.141.refs_0_), channel_id=1, source_target_pairs={{0,1},{1,0},{2,3},{3,2},{4,5},{5,4},{6,7},{7,6},{8,9},{9,8},{10,11... | collective-permute-start | bytes 258056 | tf_op jit(solution)/shard_map/ppermute | solution.py:342
  108.2 0.7 collective-permute-start.21
  109.0 0.7 collective-permute-start.22
  110.3 19.4 %collective-permute-start.23 = (f32[168,128]{1,0:T(8,128)S(1)}, f32[168,128]{1,0:T(8,128)S(1)}, u32[]{:S(2)}, u32[]{:S(2)}) collective-permute-start(f32[168,128]{1,0:T(8,128)S(1)} %get-tuple-element.151.refs_5_), channel_id=1, source_target_pairs={{0,1},{1,0},{2,3},{3,2},{4,5},{5,4},{6,7},{7,6},{8,9},{9,8},{10,11... | collective-permute-start | bytes 258056 | tf_op jit(solution)/shard_map/ppermute | solution.py:342
  134.0 3.4 %collective-permute-start.24 = (f32[32,512]{1,0:T(8,128)S(1)}, f32[32,512]{1,0:T(8,128)S(1)}, u32[]{:S(2)}, u32[]{:S(2)}) collective-permute-start(f32[32,512]{1,0:T(8,128)S(1)} %get-tuple-element.155), channel_id=1, source_target_pairs={{0,1},{1,0},{2,3},{3,2},{4,5},{5,4},{6,7},{7,6},{8,9},{9,8},{10,11... | collective-permute-start | bytes 196616 | tf_op jit(solution)/shard_map/ppermute | solution.py:342
  134.4 3.0 %collective-permute-start.25 = (f32[32,512]{1,0:T(8,128)S(1)}, f32[32,512]{1,0:T(8,128)S(1)}, u32[]{:S(2)}, u32[]{:S(2)}) collective-permute-start(f32[32,512]{1,0:T(8,128)S(1)} %get-tuple-element.156), channel_id=1, source_target_pairs={{1,2},{3,4},{5,6},{7,8},{9,10},{11,12},{13,14},{15,16},{17,18},{19... | collective-permute-start | bytes 196616 | tf_op jit(solution)/shard_map/ppermute | solution.py:342
  138.9 4.3 %collective-permute-start.26 = (f32[168,128]{1,0:T(8,128)S(1)}, f32[168,128]{1,0:T(8,128)S(1)}, u32[]{:S(2)}, u32[]{:S(2)}) collective-permute-start(f32[168,128]{1,0:T(8,128)S(1)} %get-tuple-element.163.refs_0_), channel_id=1, source_target_pairs={{0,1},{1,0},{2,3},{3,2},{4,5},{5,4},{6,7},{7,6},{8,9},{9,8},{10,11... | collective-permute-start | bytes 258056 | tf_op jit(solution)/shard_map/ppermute | solution.py:342
  145.8 0.7 collective-permute-start.30
  147.1 19.8 %collective-permute-start.31 = (f32[168,128]{1,0:T(8,128)S(1)}, f32[168,128]{1,0:T(8,128)S(1)}, u32[]{:S(2)}, u32[]{:S(2)}) collective-permute-start(f32[168,128]{1,0:T(8,128)S(1)} %get-tuple-element.173.refs_5_), channel_id=1, source_target_pairs={{0,1},{1,0},{2,3},{3,2},{4,5},{5,4},{6,7},{7,6},{8,9},{9,8},{10,11... | collective-permute-start | bytes 258056 | tf_op jit(solution)/shard_map/ppermute | solution.py:342
  (15 other events, 27.1 us)
